TPU v7x, 32 devices: a whole 2x2x4 slice. The times are simulated.
32 devices in a mesh: row: 4 (over z), col: 8 (over y, x, core).
Axes of the slice: x: 2, y: 2, z: 4, core: 2. Of those that a mesh axis runs over, the one named last changes fastest.
Arguments:
- hidden_in: bfloat16 [1536, 2, 7168], P('row', None, 'col'), may hold values from -16 to 16
- final_gain: float32 [2, 7168], P(None, 'col'), may hold values from 0.25 to 1.75
- unembed: bfloat16 [7168, 32768], P('row', 'col'), may hold values from -2 to 2
- lengths: int32 [8], replicated, may hold values from 1 to 768, 1536 in all
- targets: int32 [1536], P('row'), may hold values from 0 to 32767
- owner: int32 [8], replicated, may hold values from 0 to 7
Outputs:
- owner_table: float32 [8, 3, 8], P('col')
Inputs may be any that keep to these rules, and one draw needn't show every extreme that they name: The lengths sum to 1536; the longest is exactly 768.
All inputs are finite; a program needn't handle non-finite values.
Results may differ from a plain program's by a relative error of at most 0.00056.
Values may be sent and summed in bfloat16 or wider, within the bound.
A program may use at most 192 MiB of HBM per device.

v0:
```python
import jax
import jax.numpy as jnp
from jax import lax
from jax.sharding import PartitionSpec as P

EPS = 1e-05


def per_device(n_row, n_col, hidden_in, final_gain, unembed, lengths, targets, owner):
    tok_rows = hidden_in.shape[0]
    width = hidden_in.shape[2] * n_col
    vocab_cols = unembed.shape[1] // n_row
    tokens = tok_rows * n_row
    row_index = lax.axis_index("row")
    col_index = lax.axis_index("col")
    stream = hidden_in.astype(jnp.float32)
    square_sum = lax.psum(jnp.sum(stream * stream, axis=2), "col")
    normed = (
        stream * lax.rsqrt(square_sum[:, :, None] / width + EPS) * final_gain[None, :, :]
    ).astype(jnp.bfloat16)
    normed = normed.reshape(tok_rows * 2, hidden_in.shape[2])
    columns = lax.all_to_all(unembed, "row", split_axis=1, concat_axis=0, tiled=True)
    features = lax.all_gather(normed, "row", axis=0, tiled=True)
    features = lax.all_gather(features, "col", axis=0, tiled=False)
    features = features.transpose(1, 0, 2).reshape(tokens * 2, width)
    logits = jnp.dot(features, columns, preferred_element_type=jnp.float32)
    row_max = jnp.max(logits, axis=1)
    exp_total = jnp.sum(jnp.exp(logits - row_max[:, None]), axis=1)
    all_targets = lax.all_gather(targets, "row", axis=0, tiled=True)
    first = (col_index * n_row + row_index) * vocab_cols
    vocab_ids = first + jnp.arange(vocab_cols, dtype=jnp.int32)
    wanted = jnp.repeat(all_targets, 2)
    picked = jnp.sum(jnp.where(wanted[:, None] == vocab_ids[None, :], logits, 0.0), axis=1)
    max_logit = lax.pmax(row_max, ("row", "col"))
    exp_total, picked = lax.psum(
        (exp_total * jnp.exp(row_max - max_logit), picked), ("row", "col")
    )
    logp = (picked - (max_logit + jnp.log(exp_total))).reshape(tokens, 2)
    log_ratio = logp[:, 0] - logp[:, 1]
    token_index = jnp.arange(tokens, dtype=jnp.int32)
    seq_ends = jnp.cumsum(lengths)
    segment = jnp.sum((seq_ends[None, :] <= token_index[:, None]).astype(jnp.int32), axis=1)
    member = segment[:, None] == jnp.arange(lengths.shape[0], dtype=jnp.int32)[None, :]
    ratio_sums = jnp.sum(jnp.where(member, log_ratio[:, None], 0.0), axis=0)
    squares = jnp.sum(jnp.where(member, (log_ratio * log_ratio)[:, None], 0.0), axis=0)
    ratio_max = jnp.max(jnp.where(member, log_ratio[:, None], -1e30), axis=0)
    seq_stats = jnp.stack([ratio_sums, squares, ratio_max])
    owned = owner == col_index
    return jnp.where(owned[None, :], seq_stats, 0.0)[None]


def solution(mesh):
    import functools
    in_specs = (P("row", None, "col"), P(None, "col"), P("row", "col"), P(), P("row"), P())
    return jax.shard_map(
        functools.partial(per_device, mesh.shape["row"], mesh.shape["col"]),
        mesh=mesh,
        in_specs=in_specs,
        out_specs=P("col", None, None),
        check_vma=False,
    )
```

profile of v0, /device:TPU:0, one launch (start us, length us, event | category | flops | bytes accessed | tf_op | source)
XLA Modules:
  0.0 707.7 jit_solution(4782669329813629759)
XLA Ops:
  6.5 2.8 fusion
  9.4 0.1 copy.26
  9.5 15.1 %psum.21 = f32[384,2]{0,1:T(2,128)S(1)} all-reduce(f32[384,2]{0,1:T(2,128)S(1)} %copy.26), channel_id=1, replica_groups=mesh['row'=4,'col'=8] {'col'}, use_global_device_ids=true, to_apply=%region_3.0 | all-reduce | flops 768 | bytes 6144 | tf_op jit(solution)/shard_map/psum | solution.py:17
  24.6 0.1 copy.27
  24.8 2.8 fusion.2
  27.6 1.4 reshape.117
  29.1 101.9 %all-gather.5.cloned.1.call-done = bf16[3072,896]{1,0:T(8,128)(2,1)} async-done(((bf16[768,896]{1,0:T(8,128)(2,1)}), bf16[3072,896]{1,0:T(8,128)(2,1)}) %all-gather.5.cloned.1.call-update) | async-done | bytes 5505040 | tf_op jit(solution)/shard_map/all_gather | solution.py:23
  131.0 19.8 %copy.29 = bf16[1792,4096]{0,1:T(8,128)(2,1)} copy(bf16[1792,4096]{1,0:T(8,128)(2,1)} %param.8) | data formatting | bytes 29360128 | tf_op args[2]
  150.7 6.9 all-to-all-start
  157.7 323.5 %all-gather.1 = s32[4,1,384]{2,1,0:T(1,128)S(1)} all-gather(s32[1,1,384]{2,1,0:T(1,128)S(1)} %reshape.121), channel_id=1, replica_groups=mesh['row'=4,'col'=8] {'row'}, dimensions={0}, use_global_device_ids=true | all-gather | bytes 7680 | tf_op jit(solution)/shard_map/all_gather | solution.py:29
  481.2 0.3 broadcast_in_dim.61
  481.5 0.4 eq.39
  481.8 0.2 reduce-window.8
  482.0 0.1 convert_reduce_fusion
  482.2 18.7 %copy.30 = bf16[4,1792,1024]{2,1,0:T(8,128)(2,1)} copy(bf16[4,1792,1024]{1,2,0:T(8,128)(2,1)} %bitcast.6) | data formatting | bytes 29360128 | tf_op jit(solution)/shard_map/all_to_all | solution.py:22
  500.9 56.7 %copy.28 = bf16[3072,8,896]{0,2,1:T(8,128)(2,1)} copy(bf16[3072,8,896]{2,0,1:T(8,128)(2,1)} %bitcast.15) | data formatting | bytes 88080384 | tf_op jit(solution)/shard_map/transpose | solution.py:25
  557.5 54.9 %fusion.4 = (f32[3072]{0:T(1024)S(1)}, f32[3072,1024]{0,1:T(8,128)}) fusion(bf16[3072,7168]{0,1:T(8,128)(2,1)} %bitcast.16, bf16[7168,1024]{1,0:T(8,128)(2,1)} %bitcast.17), kind=kOutput, calls=%fused_computation.22 | convolution fusion | flops 45100298240 | bytes 71315456 | tf_op jit(solution)/shard_map/dot_general | solution.py:26
  612.4 37.9 %pmax.7 = f32[3072]{0:T(1024)S(1)} all-reduce(f32[3072]{0:T(1024)S(1)} %get-tuple-element.14), channel_id=1, replica_groups=mesh['row'=4,'col'=8] {'row','col'}, use_global_device_ids=true, to_apply=%region_7.8 | all-reduce | flops 3072 | bytes 24576 | tf_op jit(solution)/shard_map/pmax | solution.py:34
  650.3 6.6 exponential_reduce_fusion
  656.9 41.7 %all-reduce = (f32[3072]{0:T(1024)S(1)}, f32[3072]{0:T(1024)S(1)}) all-reduce(f32[3072]{0:T(1024)S(1)} %get-tuple-element.6, f32[3072]{0:T(1024)S(1)} %exponential_multiply_fusion), channel_id=1, replica_groups=mesh['row'=4,'col'=8] {'row','col'}, use_global_device_ids=true, to_apply=%region_5.6 | all-reduce | flops 6144 | bytes 49152 | tf_op jit(solution)/shard_map/psum | solution.py:35
  698.7 0.7 reshape.119
  699.5 0.7 multiply_reduce_fusion
  700.2 0.2 select_reduce_fusion.3
  700.3 0.6 copy.31
  (21 shorter events, 0.2 us)
Async XLA Ops:
  6.5 124.4 %all-gather.5.cloned.1.call-start = ((), (), s32[]{:S(2)}) async-start(), calls=%async_computation.1 | async-start | bytes 6881280 | tf_op jit(solution)/shard_map/all_gather | solution.py:23
  29.0 471.9 %all-gather.7.cloned.1.call-start = ((), (), s32[]{:S(2)}) async-start(), calls=%async_computation.2 | async-start | bytes 49545216 | tf_op jit(solution)/shard_map/all_gather | solution.py:24
  150.7 6.9 copy-start
  150.7 331.1 %copy-start.1 = (s32[8]{0:T(128)S(1)}, s32[8]{0:T(128)}, u32[]{:S(2)}) copy-start(s32[8]{0:T(128)} %param.9) | copy-start | bytes 100
  150.7 331.4 %copy-start.2 = (s32[8]{0:T(128)S(1)}, s32[8]{0:T(128)}, u32[]{:S(2)}) copy-start(s32[8]{0:T(128)} %param.11) | copy-start | bytes 100
  150.7 331.4 %all-to-all-start = ((bf16[1792,4,1024]{0,2,1:T(8,128)(2,1)}), bf16[1792,4,1024]{0,2,1:T(8,128)(2,1)}, u32[]{:S(2)}, u32[]{:S(2)}) async-start(bf16[1792,4,1024]{0,2,1:T(8,128)(2,1)} %bitcast.14), calls=%async_computation | async-start | bytes 29360128 | tf_op jit(solution)/shard_map/all_to_all | solution.py:22
Sparse Core Ops, SparseCore 0:
  29.1 101.7 all-gather.4
  132.8 204.2 all-gather.6
where the time goes:
time: 711 us; the launch traced here: 708 us
  blocking collectives  418 us (59%)
  waiting for transfers between devices  102 us (14%)
  local copies, waits for them, and re-layouts  98.7 us (14%)
  matrix products  54.9 us (8%)
  other arithmetic  13.5 us (2%)
  between operations  13.5 us (2%)
    all_gather x1, blocking collectives, per_device(): all_targets = lax.all_gather(targets, 'row', axis=0, tiled=True)  324 us
    all_gather x1, waiting for transfers between devices, per_device(): features = lax.all_gather(normed, 'row', axis=0, tiled=True)  102 us
    transpose x1, local copies, waits for them, and re-layouts, per_device(): features = features.transpose(1, 0, 2).reshape(tokens * 2, width)  56.7 us
    dot_general x1, matrix products, per_device(): logits = jnp.dot(features, columns, preferred_element_type=jnp.float32)  54.9 us
    psum x1, blocking collectives, per_device(): lax.psum((exp_total * jnp.exp(row_max - max_logit), picked), ('row', 'col'))  41.7 us
    pmax x1, blocking collectives, per_device(): max_logit = lax.pmax(row_max, ('row', 'col'))  37.9 us
    unnamed x9, local copies, waits for them, and re-layouts  19.8 us
    all_to_all x1, local copies, waits for them, and re-layouts, per_device(): lax.all_to_all(unembed, 'row', split_axis=1, concat_axis=0, tiled=True)  18.7 us
  transfers between devices with their start and end apart: 3, of which 1 were waited for; matrix products, arithmetic and copies ran while one was open for 6% of the time, Pallas kernels for 0%

commit v1 on v0

--- a/solution.py
+++ b/solution.py
@@ -1,9 +1,75 @@
+import functools
+
 import jax
 import jax.numpy as jnp
 from jax import lax
+from jax.experimental import pallas as pl
+from jax.experimental.pallas import tpu as pltpu
 from jax.sharding import PartitionSpec as P
 
 EPS = 1e-05
+LANES = 128
+
+
+def score_kernel(n_row, row_ref, features_ref, wanted_ref, *refs):
+    pieces, stats_ref = refs[:-1], refs[-1]
+    blocks, rows, depth = features_ref.shape
+    vocab_cols = pieces[0].shape[1]
+    share = blocks // n_row
+    logits = jnp.zeros((rows, vocab_cols), jnp.float32)
+    for shift in range(n_row):
+        source = lax.rem(row_ref[0] + n_row - shift, n_row)
+        for part in range(share):
+            logits += jnp.dot(
+                features_ref[source * share + part],
+                pieces[shift][pl.ds(part * depth, depth), :],
+                preferred_element_type=jnp.float32,
+            )
+    row_max = jnp.max(logits, axis=1, keepdims=True)
+    exp_total = jnp.sum(jnp.exp(logits - row_max), axis=1, keepdims=True)
+    vocab_ids = lax.broadcasted_iota(jnp.int32, (rows, vocab_cols), 1)
+    picked = jnp.sum(
+        jnp.where(wanted_ref[...] == vocab_ids, logits, 0.0), axis=1, keepdims=True
+    )
+    lane = lax.broadcasted_iota(jnp.int32, (rows, LANES), 1)
+    stats_ref[...] = jnp.where(lane == 0, row_max, jnp.where(lane == 1, exp_total, picked))
+
+
+def score(n_row, row_index, features, pieces, wanted):
+    blocks, tokens, depth = features.shape
+    vocab_cols = pieces[0].shape[1]
+    rows = 256
+    return pl.pallas_call(
+        functools.partial(score_kernel, n_row),
+        grid=(tokens // rows,),
+        out_shape=jax.ShapeDtypeStruct((tokens, LANES), jnp.float32),
+        in_specs=[
+            pl.BlockSpec(memory_space=pltpu.SMEM),
+            pl.BlockSpec((blocks, rows, depth), lambda i: (0, i, 0)),
+            pl.BlockSpec((rows, 1), lambda i: (i, 0)),
+            *(pl.BlockSpec(piece.shape, lambda i: (0, 0)) for piece in pieces),
+        ],
+        out_specs=pl.BlockSpec((rows, LANES), lambda i: (i, 0)),
+        compiler_params=pltpu.CompilerParams(vmem_limit_bytes=56 << 20),
+        cost_estimate=pl.CostEstimate(
+            flops=2 * tokens * blocks * depth * vocab_cols,
+            bytes_accessed=2 * (features.size + n_row * pieces[0].size),
+            transcendentals=tokens * vocab_cols,
+        ),
+    )(row_index[None], features, wanted, *pieces)
+
+
+def cut_columns(n_row, row_index, unembed, vocab_cols):
+    return [
+        lax.dynamic_slice_in_dim(
+            unembed, lax.rem(row_index + k, n_row) * vocab_cols, vocab_cols, axis=1
+        )
+        for k in range(n_row)
+    ]
+
+
+def send_on(n_row, shift, piece):
+    return lax.ppermute(piece, "row", [(r, (r + shift) % n_row) for r in range(n_row)])
 
 
 def per_device(n_row, n_col, hidden_in, final_gain, unembed, lengths, targets, owner):
@@ -19,22 +85,20 @@
         stream * lax.rsqrt(square_sum[:, :, None] / width + EPS) * final_gain[None, :, :]
     ).astype(jnp.bfloat16)
     normed = normed.reshape(tok_rows * 2, hidden_in.shape[2])
-    columns = lax.all_to_all(unembed, "row", split_axis=1, concat_axis=0, tiled=True)
+    cuts = cut_columns(n_row, row_index, unembed, vocab_cols)
+    normed, *cuts = lax.optimization_barrier((normed, *cuts))
+    nearest = send_on(n_row, 1, cuts[1])
     features = lax.all_gather(normed, "row", axis=0, tiled=True)
+    features, nearest = lax.optimization_barrier((features, nearest))
+    pieces = [cuts[0], nearest, *(send_on(n_row, k, cuts[k]) for k in range(2, n_row))]
     features = lax.all_gather(features, "col", axis=0, tiled=False)
-    features = features.transpose(1, 0, 2).reshape(tokens * 2, width)
-    logits = jnp.dot(features, columns, preferred_element_type=jnp.float32)
-    row_max = jnp.max(logits, axis=1)
-    exp_total = jnp.sum(jnp.exp(logits - row_max[:, None]), axis=1)
-    all_targets = lax.all_gather(targets, "row", axis=0, tiled=True)
+    wanted = jnp.repeat(lax.all_gather(targets, "row", axis=0, tiled=True), 2)
     first = (col_index * n_row + row_index) * vocab_cols
-    vocab_ids = first + jnp.arange(vocab_cols, dtype=jnp.int32)
-    wanted = jnp.repeat(all_targets, 2)
-    picked = jnp.sum(jnp.where(wanted[:, None] == vocab_ids[None, :], logits, 0.0), axis=1)
-    max_logit = lax.pmax(row_max, ("row", "col"))
-    exp_total, picked = lax.psum(
-        (exp_total * jnp.exp(row_max - max_logit), picked), ("row", "col")
-    )
+    stats = score(n_row, row_index, features, pieces, (wanted - first)[:, None])
+    stats = lax.all_gather(stats[:, :3].T, ("row", "col"), axis=0, tiled=False)
+    max_logit = jnp.max(stats[:, 0], axis=0)
+    exp_total = jnp.sum(stats[:, 1] * jnp.exp(stats[:, 0] - max_logit[None]), axis=0)
+    picked = jnp.sum(stats[:, 2], axis=0)
     logp = (picked - (max_logit + jnp.log(exp_total))).reshape(tokens, 2)
     log_ratio = logp[:, 0] - logp[:, 1]
     token_index = jnp.arange(tokens, dtype=jnp.int32)
@@ -50,7 +114,6 @@
 
 
 def solution(mesh):
-    import functools
     in_specs = (P("row", None, "col"), P(None, "col"), P("row", "col"), P(), P("row"), P())
     return jax.shard_map(
         functools.partial(per_device, mesh.shape["row"], mesh.shape["col"]),

time: 711 us -> 590 us (0.83)
  blocking collectives: 418 us -> 256 us
  waiting for transfers between devices: 102 us -> 223 us
  local copies, waits for them, and re-layouts: 98.7 us -> 18.3 us
  Pallas kernels: 0 us -> 64.4 us
  matrix products: 54.9 us -> 0 us
    ppermute x0 -> x3, waiting for transfers between devices: none -> 152 us  [send_on(): lax.ppermute(piece, 'row', [(r, (r + shift) % n_row) for r in range(n_row)])]
    all_gather x1, waiting for transfers between devices: 102 us -> 17.1 us  [per_device(): features = lax.all_gather(normed, 'row', axis=0, tiled=True)]
    all_gather x1, blocking collectives: 324 us -> 241 us  [per_device(): wanted = jnp.repeat(lax.all_gather(targets, 'row', axis=0, tiled=True), 2)]
    pallas_call x0 -> x1, Pallas kernels: none -> 64.4 us  [score(): pl.pallas_call(functools.partial(score_kernel, n_row), grid=(tokens // ro...]
    transpose x1 -> x0, local copies, waits for them, and re-layouts: 56.7 us -> none  [per_device(): features = features.transpose(1, 0, 2).reshape(tokens * 2, width)]
    dot_general x1 -> x0, matrix products: 54.9 us -> none  [per_device(): logits = jnp.dot(features, columns, preferred_element_type=jnp.float32)]
    all_gather x0 -> x1, waiting for transfers between devices: none -> 54.7 us  [per_device(): stats = lax.all_gather(stats[:, :3].T, ('row', 'col'), axis=0, tiled=False)]
    psum x1 -> x0, blocking collectives: 41.7 us -> none  [per_device(): lax.psum((exp_total * jnp.exp(row_max - max_logit), picked), ('row', 'col'))]
  transfers between devices with their start and end apart: 3 -> 6, of which waited for: 1 -> 3; matrix products, arithmetic and copies ran while one was open for 6% -> 0% of each run, Pallas kernels for 0% -> 0%
where the time goes in v1:
time: 590 us; the launch traced here: 589 us
  blocking collectives  256 us (43%)
  waiting for transfers between devices  223 us (38%)
  Pallas kernels  64.4 us (11%)
  local copies, waits for them, and re-layouts  18.3 us (3%)
  between operations  13.2 us (2%)
  other arithmetic  10.3 us (2%)
    all_gather x1, blocking collectives, per_device(): wanted = jnp.repeat(lax.all_gather(targets, 'row', axis=0, tiled=True), 2)  241 us
    ppermute x3, waiting for transfers between devices, send_on(): lax.ppermute(piece, 'row', [(r, (r + shift) % n_row) for r in range(n_row)])  152 us
    pallas_call x1, Pallas kernels, score(): pl.pallas_call(functools.partial(score_kernel, n_row), grid=(tokens // ro...  64.4 us
    all_gather x1, waiting for transfers between devices, per_device(): stats = lax.all_gather(stats[:, :3].T, ('row', 'col'), axis=0, tiled=False)  54.7 us
    all_gather x1, waiting for transfers between devices, per_device(): features = lax.all_gather(normed, 'row', axis=0, tiled=True)  17.1 us
    psum x1, blocking collectives, per_device(): square_sum = lax.psum(jnp.sum(stream * stream, axis=2), 'col')  15.1 us
  transfers between devices with their start and end apart: 6, of which 3 were waited for; matrix products, arithmetic and copies ran while one was open for 0% of the time, Pallas kernels for 0%

profile of v1, /device:TPU:0, one launch (start us, length us, event | category | flops | bytes accessed | tf_op | source)
XLA Modules:
  0.0 589.4 jit_solution(13290230008073541266)
XLA Ops:
  6.5 2.9 fusion
  9.6 15.1 %psum.7 = f32[384,2]{0,1:T(2,128)S(1)} all-reduce(f32[384,2]{0,1:T(2,128)S(1)} %copy.29), channel_id=1, replica_groups=mesh['row'=4,'col'=8] {'col'}, use_global_device_ids=true, to_apply=%region_3.0 | all-reduce | flops 768 | bytes 6144 | tf_op jit(solution)/shard_map/psum | solution.py:83
  24.9 2.2 fusion.2
  27.1 1.4 reshape.123
  28.5 11.0 %constant_dynamic-slice_fusion = (bf16[1792,1024]{1,0:T(8,128)(2,1)}, bf16[1792,1024]{1,0:T(8,128)(2,1)}, bf16[1792,1024]{1,0:T(8,128)(2,1)}, bf16[1792,1024]{1,0:T(8,128)(2,1)}) fusion(bf16[1792,4096]{1,0:T(8,128)(2,1)} %param.8, s32[]{:T(128)S(6)} %select_n.36, s32[]{:T(128)S(6)} %select_n.34, s32[]{:T(128)S(6)} %select_n.33, s32[]{:T(128)S(6)} %select_n.35), kind=kLoop, calls=%fused_computation.26 | loop fusion | bytes 29360144 | tf_op jit(solution)/shard_map/dynamic_slice | solution.py:64
  39.5 1.6 collective-permute-start
  41.1 151.5 %collective-permute-done.refs_1_ = bf16[1792,1024]{1,0:T(8,128)(2,1)} collective-permute-done((bf16[1792,1024]{1,0:T(8,128)(2,1)}, bf16[1792,1024]{1,0:T(8,128)(2,1)}, u32[]{:S(2)}, u32[]{:S(2)}) %collective-permute-start) | collective-permute-done | bytes 3670048 | tf_op jit(solution)/shard_map/ppermute | solution.py:72
  192.6 17.1 %all-gather.8.cloned.1.call-done = bf16[3072,896]{1,0:T(8,128)(2,1)} async-done(((bf16[768,896]{1,0:T(8,128)(2,1)}), bf16[3072,896]{1,0:T(8,128)(2,1)}) %all-gather.8.cloned.1.call-update) | async-done | bytes 5505040 | tf_op jit(solution)/shard_map/all_gather | solution.py:91
  209.8 0.8 collective-permute-start.1
  210.6 1.4 collective-permute-start.2
  212.0 240.8 %all-gather.2 = s32[4,1,384]{2,1,0:T(1,128)S(1)} all-gather(s32[1,1,384]{2,1,0:T(1,128)S(1)} %reshape.126), channel_id=1, replica_groups=mesh['row'=4,'col'=8] {'row'}, dimensions={0}, use_global_device_ids=true | all-gather | bytes 7680 | tf_op jit(solution)/shard_map/all_gather | solution.py:95
  452.8 0.3 broadcast_in_dim.61
  453.1 1.5 sub.46.wanted_ref
  454.6 64.4 %shard_map.64 = f32[3072,128]{1,0:T(8,128)} custom-call(s32[1]{0:T(128)} %bitcast.2.row_ref, bf16[8,3072,896]{2,1,0:T(8,128)(2,1)} %bitcast.29, s32[3072,1]{1,0:T(8,128)} %sub.46.wanted_ref, bf16[1792,1024]{1,0:T(8,128)(2,1)} %get-tuple-element.15.refs_0_, bf16[1792,1024]{1,0:T(8,128)(2,1)} %collective-permute-done.refs_1_, ...), custom_call_target="tpu_custom_call" | custom-call | flops 45097156608 | bytes 58720256 | tf_op jit(solution)/shard_map/pallas_call | solution.py:42
  519.0 1.5 slice_bitcast_fusion
  520.5 1.1 copy.32
  521.6 0.2 reduce-window.8
  521.9 54.7 %all-gather.12.cloned.1.call-done = f32[32,3,3072]{2,1,0:T(4,128)} async-done(((f32[1,3,3072]{2,1,0:T(4,128)}), f32[32,3,3072]{2,1,0:T(4,128)}) %all-gather.12.cloned.1.call-update) | async-done | bytes 1179664 | tf_op jit(solution)/shard_map/all_gather | solution.py:98
  576.6 3.9 slice_reduce_fusion.1
  580.5 0.2 fusion.4
  580.7 0.7 sub.43
  581.4 0.7 multiply_reduce_fusion
  582.1 0.2 select_reduce_fusion.2
  582.3 0.6 copy.35
  (27 shorter events, 0.6 us)
Async XLA Ops:
  6.5 18.3 %copy-start = (bf16[384,2,896]{2,1,0:T(2,128)(2,1)S(1)}, bf16[384,2,896]{2,1,0:T(2,128)(2,1)}, u32[]{:S(2)}) copy-start(bf16[384,2,896]{2,1,0:T(2,128)(2,1)} %param.6) | copy-start | bytes 4128772
  6.5 203.2 %all-gather.8.cloned.1.call-start = ((), (), s32[]{:S(2)}) async-start(), calls=%async_computation | async-start | bytes 6881280 | tf_op jit(solution)/shard_map/all_gather | solution.py:91
  39.4 415.1 %all-gather.10.cloned.1.call-start = ((), (), s32[]{:S(2)}) async-start(), calls=%async_computation.1 | async-start | bytes 49545216 | tf_op jit(solution)/shard_map/all_gather | solution.py:94
  39.5 153.1 %collective-permute-start = (bf16[1792,1024]{1,0:T(8,128)(2,1)}, bf16[1792,1024]{1,0:T(8,128)(2,1)}, u32[]{:S(2)}, u32[]{:S(2)}) collective-permute-start(bf16[1792,1024]{1,0:T(8,128)(2,1)} %get-tuple-element.13), channel_id=1, source_target_pairs={{0,8},{8,16},{16,24},{24,0},{1,9},{9,17},{17,25},{25,1},{2,10},{10... | collective-permute-start | bytes 11010056 | tf_op jit(solution)/shard_map/ppermute | solution.py:72
  209.8 2.2 copy-start.1
  209.8 366.8 %all-gather.12.cloned.1.call-start = ((), (), s32[]{:S(2)}) async-start(), calls=%async_computation.2 | async-start | bytes 1622016 | tf_op jit(solution)/shard_map/all_gather | solution.py:98
  209.8 244.7 %collective-permute-start.1 = (bf16[1792,1024]{1,0:T(8,128)(2,1)}, bf16[1792,1024]{1,0:T(8,128)(2,1)}, u32[]{:S(2)}, u32[]{:S(2)}) collective-permute-start(bf16[1792,1024]{1,0:T(8,128)(2,1)} %get-tuple-element.17), channel_id=1, source_target_pairs={{0,16},{8,24},{16,0},{24,8},{1,17},{9,25},{17,1},{25,9},{2,18},{10... | collective-permute-start | bytes 11010056 | tf_op jit(solution)/shard_map/ppermute | solution.py:72
  210.6 244.0 %collective-permute-start.2 = (bf16[1792,1024]{1,0:T(8,128)(2,1)}, bf16[1792,1024]{1,0:T(8,128)(2,1)}, u32[]{:S(2)}, u32[]{:S(2)}) collective-permute-start(bf16[1792,1024]{1,0:T(8,128)(2,1)} %get-tuple-element.18), channel_id=1, source_target_pairs={{0,24},{8,0},{16,8},{24,16},{1,25},{9,1},{17,9},{25,17},{2,26},{10... | collective-permute-start | bytes 11010056 | tf_op jit(solution)/shard_map/ppermute | solution.py:72
  519.0 2.7 copy-start.2
  519.0 2.9 copy-start.3
Sparse Core Ops, SparseCore 0:
  39.6 170.1 all-gather.7
  211.7 203.5 all-gather.9
  521.7 54.8 all-gather.11

commit v2 on v1

--- a/solution.py
+++ b/solution.py
@@ -11,18 +11,18 @@
 LANES = 128
 
 
-def score_kernel(n_row, row_ref, features_ref, wanted_ref, *refs):
+def score_kernel(n_row, spans, row_ref, features_ref, wanted_ref, *refs):
     pieces, stats_ref = refs[:-1], refs[-1]
     blocks, rows, depth = features_ref.shape
     vocab_cols = pieces[0].shape[1]
     share = blocks // n_row
     logits = jnp.zeros((rows, vocab_cols), jnp.float32)
-    for shift in range(n_row):
+    for (shift, first), piece in zip(spans, pieces):
         source = lax.rem(row_ref[0] + n_row - shift, n_row)
-        for part in range(share):
+        for part in range(piece.shape[0] // depth):
             logits += jnp.dot(
-                features_ref[source * share + part],
-                pieces[shift][pl.ds(part * depth, depth), :],
+                features_ref[source * share + first + part],
+                piece[pl.ds(part * depth, depth), :],
                 preferred_element_type=jnp.float32,
             )
     row_max = jnp.max(logits, axis=1, keepdims=True)
@@ -35,12 +35,12 @@
     stats_ref[...] = jnp.where(lane == 0, row_max, jnp.where(lane == 1, exp_total, picked))
 
 
-def score(n_row, row_index, features, pieces, wanted):
+def score(n_row, row_index, features, spans, pieces, wanted):
     blocks, tokens, depth = features.shape
     vocab_cols = pieces[0].shape[1]
     rows = 256
     return pl.pallas_call(
-        functools.partial(score_kernel, n_row),
+        functools.partial(score_kernel, n_row, spans),
         grid=(tokens // rows,),
         out_shape=jax.ShapeDtypeStruct((tokens, LANES), jnp.float32),
         in_specs=[
@@ -53,7 +53,7 @@
         compiler_params=pltpu.CompilerParams(vmem_limit_bytes=56 << 20),
         cost_estimate=pl.CostEstimate(
             flops=2 * tokens * blocks * depth * vocab_cols,
-            bytes_accessed=2 * (features.size + n_row * pieces[0].size),
+            bytes_accessed=2 * (features.size + sum(piece.size for piece in pieces)),
             transcendentals=tokens * vocab_cols,
         ),
     )(row_index[None], features, wanted, *pieces)
@@ -80,21 +80,27 @@
     row_index = lax.axis_index("row")
     col_index = lax.axis_index("col")
     stream = hidden_in.astype(jnp.float32)
-    square_sum = lax.psum(jnp.sum(stream * stream, axis=2), "col")
+    cuts = cut_columns(n_row, row_index, unembed, vocab_cols)
+    split = max(1, n_col // n_row // 2) * hidden_in.shape[2]
+    cuts = [cuts[0], cuts[1][:split], cuts[1][split:], *cuts[2:]]
+    square_sum, *cuts = lax.optimization_barrier((jnp.sum(stream * stream, axis=2), *cuts))
+    square_sum = lax.psum(square_sum, "col")
     normed = (
         stream * lax.rsqrt(square_sum[:, :, None] / width + EPS) * final_gain[None, :, :]
     ).astype(jnp.bfloat16)
     normed = normed.reshape(tok_rows * 2, hidden_in.shape[2])
-    cuts = cut_columns(n_row, row_index, unembed, vocab_cols)
-    normed, *cuts = lax.optimization_barrier((normed, *cuts))
-    nearest = send_on(n_row, 1, cuts[1])
+    normed, early = lax.optimization_barrier((normed, send_on(n_row, 1, cuts[1])))
+    late = send_on(n_row, 1, cuts[2])
     features = lax.all_gather(normed, "row", axis=0, tiled=True)
-    features, nearest = lax.optimization_barrier((features, nearest))
-    pieces = [cuts[0], nearest, *(send_on(n_row, k, cuts[k]) for k in range(2, n_row))]
+    features, late = lax.optimization_barrier((features, late))
+    others = [send_on(n_row, k, cuts[k + 1]) for k in range(2, n_row)]
+    pieces = [cuts[0], early, late, *others]
+    spans = [(0, 0), (1, 0), (1, split // hidden_in.shape[2])]
+    spans += [(k, 0) for k in range(2, n_row)]
     features = lax.all_gather(features, "col", axis=0, tiled=False)
     wanted = jnp.repeat(lax.all_gather(targets, "row", axis=0, tiled=True), 2)
     first = (col_index * n_row + row_index) * vocab_cols
-    stats = score(n_row, row_index, features, pieces, (wanted - first)[:, None])
+    stats = score(n_row, row_index, features, spans, pieces, (wanted - first)[:, None])
     stats = lax.all_gather(stats[:, :3].T, ("row", "col"), axis=0, tiled=False)
     max_logit = jnp.max(stats[:, 0], axis=0)
     exp_total = jnp.sum(stats[:, 1] * jnp.exp(stats[:, 0] - max_logit[None]), axis=0)

time: 590 us -> 579 us (0.981)
  waiting for transfers between devices: 223 us -> 211 us
    ppermute x3 -> x4, waiting for transfers between devices: 152 us -> 100 us  [send_on(): lax.ppermute(piece, 'row', [(r, (r + shift) % n_row) for r in range(n_row)])]
    all_gather x1, waiting for transfers between devices: 17.1 us -> 56.9 us  [per_device(): features = lax.all_gather(normed, 'row', axis=0, tiled=True)]
  transfers between devices with their start and end apart: 6 -> 7, of which waited for: 3 -> 4; matrix products, arithmetic and copies ran while one was open for 0% -> 1% of each run, Pallas kernels for 0% -> 0%
where the time goes in v2:
time: 579 us
  blocking collectives  256 us (44%)
  waiting for transfers between devices  211 us (36%)
  Pallas kernels  64.4 us (11%)
  local copies, waits for them, and re-layouts  20.5 us (4%)
  between operations  13.3 us (2%)
  other arithmetic  9.54 us (2%)
    all_gather x1, blocking collectives, per_device(): wanted = jnp.repeat(lax.all_gather(targets, 'row', axis=0, tiled=True), 2)  242 us
    ppermute x4, waiting for transfers between devices, send_on(): lax.ppermute(piece, 'row', [(r, (r + shift) % n_row) for r in range(n_row)])  100 us
    pallas_call x1, Pallas kernels, score(): pl.pallas_call(functools.partial(score_kernel, n_row, spans), grid=(token...  64.4 us
    all_gather x1, waiting for transfers between devices, per_device(): features = lax.all_gather(normed, 'row', axis=0, tiled=True)  56.9 us
    all_gather x1, waiting for transfers between devices, per_device(): stats = lax.all_gather(stats[:, :3].T, ('row', 'col'), axis=0, tiled=False)  53.9 us
    psum x1, blocking collectives, per_device(): square_sum = lax.psum(square_sum, 'col')  14.2 us
  transfers between devices with their start and end apart: 7, of which 4 were waited for; matrix products, arithmetic and copies ran while one was open for 1% of the time, Pallas kernels for 0%

profile of v2, /device:TPU:0, one launch (start us, length us, event | category | flops | bytes accessed | tf_op | source)
XLA Modules:
  0.0 579.2 jit_solution(3191201290989668357)
XLA Ops:
  6.5 2.8 fusion
  9.4 4.4 fusion.8
  13.8 8.8 %constant_dynamic-slice_fusion.1 = (bf16[1792,1024]{1,0:T(8,128)(2,1)}, bf16[1792,1024]{1,0:T(8,128)(2,1)}, bf16[1792,1024]{1,0:T(8,128)(2,1)}) fusion(bf16[1792,4096]{1,0:T(8,128)(2,1)} %param.8, s32[]{:T(128)S(6)} %select_n.36, s32[]{:T(128)S(6)} %select_n.33, s32[]{:T(128)S(6)} %select_n.35), kind=kLoop, calls=%fused_computation.27 | loop fusion | bytes 22020108 | tf_op jit(solution)/shard_map/dynamic_slice | solution.py:64
  22.5 3.0 collective-permute-start
  25.6 14.2 %psum.7 = f32[384,2]{0,1:T(2,128)S(1)} all-reduce(f32[384,2]{0,1:T(2,128)S(1)} %copy.29), channel_id=1, replica_groups=mesh['row'=4,'col'=8] {'col'}, use_global_device_ids=true, to_apply=%region_3.0 | all-reduce | flops 768 | bytes 6144 | tf_op jit(solution)/shard_map/psum | solution.py:87
  40.0 1.5 fusion.2
  41.5 1.4 reshape.123
  42.9 25.0 %collective-permute-done.refs_1_ = bf16[896,1024]{1,0:T(8,128)(2,1)} collective-permute-done((bf16[896,1024]{1,0:T(8,128)(2,1)}, bf16[896,1024]{1,0:T(8,128)(2,1)}, u32[]{:S(2)}, u32[]{:S(2)}) %collective-permute-start) | collective-permute-done | bytes 1835040 | tf_op jit(solution)/shard_map/ppermute | solution.py:72
  68.1 75.5 %collective-permute-done.1.refs_2_ = bf16[896,1024]{1,0:T(8,128)(2,1)S(1)} collective-permute-done((bf16[896,1024]{1,0:T(8,128)(2,1)}, bf16[896,1024]{1,0:T(8,128)(2,1)S(1)}, u32[]{:S(2)}, u32[]{:S(2)}) %collective-permute-start.1) | collective-permute-done | bytes 1835040 | tf_op jit(solution)/shard_map/ppermute | solution.py:72
  143.5 56.9 %all-gather.8.cloned.1.call-done = bf16[3072,896]{1,0:T(8,128)(2,1)} async-done(((bf16[768,896]{1,0:T(8,128)(2,1)}), bf16[3072,896]{1,0:T(8,128)(2,1)}) %all-gather.8.cloned.1.call-update) | async-done | bytes 5505040 | tf_op jit(solution)/shard_map/all_gather | solution.py:94
  200.5 0.7 collective-permute-start.2
  201.2 0.2 collective-permute-start.3
  201.4 242.0 %all-gather.2 = s32[4,1,384]{2,1,0:T(1,128)S(1)} all-gather(s32[1,1,384]{2,1,0:T(1,128)S(1)} %reshape.126), channel_id=1, replica_groups=mesh['row'=4,'col'=8] {'row'}, dimensions={0}, use_global_device_ids=true | all-gather | bytes 7680 | tf_op jit(solution)/shard_map/all_gather | solution.py:101
  443.5 0.3 broadcast_in_dim.61
  443.7 1.5 sub.46.wanted_ref
  445.2 64.4 %shard_map.64 = f32[3072,128]{1,0:T(8,128)} custom-call(s32[1]{0:T(128)} %bitcast.2.row_ref, bf16[8,3072,896]{2,1,0:T(8,128)(2,1)} %bitcast.29, s32[3072,1]{1,0:T(8,128)} %sub.46.wanted_ref, bf16[1792,1024]{1,0:T(8,128)(2,1)} %get-tuple-element.20.refs_0_, bf16[896,1024]{1,0:T(8,128)(2,1)} %collective-permute-done.refs_1_, bf16[896,1024]{1,0:T(8,128)(2,1)} %copy-done.3, ...), custom_call_target="tpu_custom_call" | custom-call | flops 45097156608 | bytes 58720256 | tf_op jit(solution)/shard_map/pallas_call | solution.py:42
  509.6 1.5 slice_bitcast_fusion
  511.2 1.1 copy.32
  512.3 0.2 reduce-window.8
  512.6 53.9 %all-gather.12.cloned.1.call-done = f32[32,3,3072]{2,1,0:T(4,128)} async-done(((f32[1,3,3072]{2,1,0:T(4,128)}), f32[32,3,3072]{2,1,0:T(4,128)}) %all-gather.12.cloned.1.call-update) | async-done | bytes 1179664 | tf_op jit(solution)/shard_map/all_gather | solution.py:104
  566.5 3.9 slice_reduce_fusion.1
  570.5 0.7 sub.43
  571.2 0.7 multiply_reduce_fusion
  572.1 0.6 copy.35
  (34 shorter events, 0.9 us)
Async XLA Ops:
  6.5 193.9 %all-gather.8.cloned.1.call-start = ((), (), s32[]{:S(2)}) async-start(), calls=%async_computation | async-start | bytes 6881280 | tf_op jit(solution)/shard_map/all_gather | solution.py:94
  13.8 26.3 %copy-start = (bf16[384,2,896]{2,1,0:T(2,128)(2,1)S(1)}, bf16[384,2,896]{2,1,0:T(2,128)(2,1)}, u32[]{:S(2)}) copy-start(bf16[384,2,896]{2,1,0:T(2,128)(2,1)} %param.6) | copy-start | bytes 4128772
  13.8 26.3 %copy-start.1 = (f32[2,896]{1,0:T(2,128)S(1)}, f32[2,896]{1,0:T(2,128)}, u32[]{:S(2)}) copy-start(f32[2,896]{1,0:T(2,128)} %param.7) | copy-start | bytes 21508
  22.5 45.4 %collective-permute-start = (bf16[896,1024]{1,0:T(8,128)(2,1)}, bf16[896,1024]{1,0:T(8,128)(2,1)}, u32[]{:S(2)}, u32[]{:S(2)}) collective-permute-start(bf16[896,1024]{1,0:T(8,128)(2,1)} %get-tuple-element.16), channel_id=1, source_target_pairs={{0,8},{8,16},{16,24},{24,0},{1,9},{9,17},{17,25},{25,1},{2,10},{10... | collective-permute-start | bytes 5505032 | tf_op jit(solution)/shard_map/ppermute | solution.py:72
  67.9 377.3 %all-gather.10.cloned.1.call-start = ((), (), s32[]{:S(2)}) async-start(), calls=%async_computation.1 | async-start | bytes 49545216 | tf_op jit(solution)/shard_map/all_gather | solution.py:100
  68.0 75.5 %collective-permute-start.1 = (bf16[896,1024]{1,0:T(8,128)(2,1)}, bf16[896,1024]{1,0:T(8,128)(2,1)S(1)}, u32[]{:S(2)}, u32[]{:S(2)}) collective-permute-start(bf16[896,1024]{1,0:T(8,128)(2,1)} %get-tuple-element.18), channel_id=1, source_target_pairs={{0,8},{8,16},{16,24},{24,0},{1,9},{9,17},{17,25},{25,1},{2,10},{10... | collective-permute-start | bytes 5505032 | tf_op jit(solution)/shard_map/ppermute | solution.py:72
  143.5 56.9 %copy-start.3 = (bf16[896,1024]{1,0:T(8,128)(2,1)}, bf16[896,1024]{1,0:T(8,128)(2,1)S(1)}, u32[]{:S(2)}) copy-start(bf16[896,1024]{1,0:T(8,128)(2,1)S(1)} %collective-permute-done.1.refs_2_) | copy-start | bytes 5505028
  200.4 1.0 copy-start.2
  200.5 366.0 %all-gather.12.cloned.1.call-start = ((), (), s32[]{:S(2)}) async-start(), calls=%async_computation.2 | async-start | bytes 1622016 | tf_op jit(solution)/shard_map/all_gather | solution.py:104
  200.5 244.7 %collective-permute-start.2 = (bf16[1792,1024]{1,0:T(8,128)(2,1)}, bf16[1792,1024]{1,0:T(8,128)(2,1)}, u32[]{:S(2)}, u32[]{:S(2)}) collective-permute-start(bf16[1792,1024]{1,0:T(8,128)(2,1)} %get-tuple-element.23), channel_id=1, source_target_pairs={{0,16},{8,24},{16,0},{24,8},{1,17},{9,25},{17,1},{25,9},{2,18},{10... | collective-permute-start | bytes 11010056 | tf_op jit(solution)/shard_map/ppermute | solution.py:72
  201.2 244.0 %collective-permute-start.3 = (bf16[1792,1024]{1,0:T(8,128)(2,1)}, bf16[1792,1024]{1,0:T(8,128)(2,1)}, u32[]{:S(2)}, u32[]{:S(2)}) collective-permute-start(bf16[1792,1024]{1,0:T(8,128)(2,1)} %get-tuple-element.24), channel_id=1, source_target_pairs={{0,24},{8,0},{16,8},{24,16},{1,25},{9,1},{17,9},{25,17},{2,26},{10... | collective-permute-start | bytes 11010056 | tf_op jit(solution)/shard_map/ppermute | solution.py:72
  509.6 2.7 copy-start.4
  509.6 2.9 copy-start.5
Sparse Core Ops, SparseCore 0:
  68.1 132.3 all-gather.7
  202.3 203.9 all-gather.9
  512.4 54.0 all-gather.11
